TPU v7x, 512 devices: a whole 4x4x16 slice. The times are simulated.
512 devices in a mesh: seq: 128 (over z, y, core), ch: 4 (over x).
Axes of the slice: x: 4, y: 4, z: 16, core: 2. Of those that a mesh axis runs over, the one named last changes fastest.
Arguments:
- ingest: bfloat16 [131072, 4096], P('seq', 'ch'), may hold values from -6 to 6
- ingest_count: int32 [128], P('seq'), may hold values from 0 to 1024, as said below
- doc_lengths: int32 [128], replicated, may hold values from 1 to 2048, as said below
- in_weight: bfloat16 [4096, 5120], P('seq', 'ch'), may hold values from -0.09375 to 0.09375
- conv_weight: float32 [4, 5120], P(None, 'ch'), may hold values from -3 to 3
- conv_bias: float32 [5120], P('ch'), may hold values from -3 to 3
Outputs:
- conv_out: bfloat16 [65536, 5120], P('seq', 'ch')
Inputs may be any that keep to these rules, and one draw needn't show every extreme that they name: Device i keeps its valid rows in its first ingest_count[i] slots; the devices before i together hold between i * 512 - 256 and i * 512 + 256 rows, both ends reached in every draw; the first device holds 511 rows, and all devices together hold 65536 rows. `doc_lengths`: the lengths sum to 65536; the first document has exactly 2048 tokens.
All inputs are finite; a program needn't handle non-finite values.
Results may differ from a plain program's by a relative error of at most 0.012.
Values may be sent and summed in bfloat16 or wider, within the bound.
A program may use at most 128 MiB of HBM per device.

v0:
```python
import jax
import jax.numpy as jnp
from jax import lax
from jax.sharding import PartitionSpec as P


def shifted(value, axis, steps):
    count = lax.axis_size(axis)
    initial, last = (max(0, -steps), min(count, count - steps))
    return lax.ppermute(value, axis, [(source, source + steps) for source in range(initial, last)])


def carried_in(value, axis, join, neutral):
    count, mine = (lax.axis_size(axis), lax.axis_index(axis))
    pieces = lax.all_gather(value, axis)
    subtotal = jnp.full_like(value, 0) + jnp.asarray(neutral, value.dtype)

    def turn(position, subtotal):
        longer = join(subtotal, pieces[position])
        return jnp.where(position < mine, longer, subtotal)

    return lax.fori_loop(0, count - 1, turn, subtotal)


def move_rows(ingest, count, offset, first, tokens, extra):
    half = tokens // 2
    slots = ingest.shape[0]
    start = first + tokens - offset - extra
    tail = lax.dynamic_slice_in_dim(ingest, start, half + extra, 0)
    from_left = shifted(tail, "seq", 1)
    from_right = shifted(ingest[:half], "seq", -1)
    next_offset = offset + count
    buffer = jnp.concatenate([from_left, ingest, from_right], axis=0)
    places = first - extra + jnp.arange(tokens + extra, dtype=jnp.int32)
    lead = half + extra
    picks = jnp.where(
        places < offset,
        places - (first - extra),
        jnp.where(
            places < next_offset, lead + places - offset, lead + slots + places - next_offset
        ),
    )
    return jnp.take(buffer, picks.astype(jnp.int32), axis=0)


def body(ingest, ingest_count, doc_lengths, in_weight, conv_weight, conv_bias):
    tokens = ingest.shape[0] // 2
    channels = in_weight.shape[1]
    before = carried_in(
        ingest_count, "seq", lambda earlier, later: earlier + later, jnp.zeros_like(ingest_count)
    )
    offset = before[0]
    count = ingest_count[0]
    first = lax.axis_index("seq") * tokens
    extra = 3
    moved = move_rows(ingest, count, offset, first, tokens, extra)
    features = lax.all_gather(moved, "ch", axis=1, tiled=True)
    window = jnp.dot(
        features,
        lax.all_gather(in_weight, "seq", axis=0, tiled=True),
        preferred_element_type=jnp.float32,
    ).astype(jnp.bfloat16)
    values = window.astype(jnp.float32)
    starts = jnp.cumsum(doc_lengths) - doc_lengths
    places = first - 3 + jnp.arange(tokens + 3, dtype=jnp.int32)
    doc_ids = jnp.sum((places[:, None] >= starts[None, :]).astype(jnp.int32), axis=1) - 1
    here_ids = doc_ids[3:]
    total = jnp.zeros((tokens, channels), jnp.float32) + conv_bias[None, :]
    for lag in range(4):
        earlier = values[3 - lag : 3 - lag + tokens]
        same = (doc_ids[3 - lag : 3 - lag + tokens] == here_ids).astype(jnp.float32)
        total = total + conv_weight[lag][None, :] * earlier * same[:, None]
    return jax.nn.silu(total).astype(jnp.bfloat16)


def solution(mesh):
    placed = (P("seq", "ch"), P("seq"), P(), P("seq", "ch"), P(None, "ch"), P("ch"))
    return jax.shard_map(
        body, mesh=mesh, in_specs=placed, out_specs=P("seq", "ch"), check_vma=False
    )
```

profile of v0, /device:TPU:1, one launch (start us, length us, event | category | flops | bytes accessed | tf_op | source)
XLA Modules:
  0.0 486.9 jit_solution(12569060451620937295)
XLA Ops:
  7.2 1.3 dynamic-slice
  8.5 0.8 dynamic-update-slice
  9.2 30.5 %all-reduce = s32[128]{0:T(128)S(1)} all-reduce(s32[128]{0:T(128)S(1)} %dynamic-update-slice), channel_id=2, replica_groups=mesh['seq'=128,'ch'=4] {'seq'}, use_global_device_ids=true, to_apply=%add | all-reduce | flops 128 | bytes 1024
  39.7 175.2 %while.13 = (s32[]{:T(128)}, s32[1]{0:T(128)}, s32[]{:T(128)}, s32[128,1]{0,1:T(1,128)S(1)}, s32[]{:T(128)}) while((s32[]{:T(128)}, s32[1]{0:T(128)}, s32[]{:T(128)}, s32[128,1]{0,1:T(1,128)S(1)}, s32[]{:T(128)}) %tuple.40), condition=%wide.region_1.2_spmd, body=%wide.region_0.1_spmd.sunk | while | flops 5 | bytes 107 | solution.py:22
  41.1 0.7 constant_dynamic-slice_fusion.3
  42.5 0.7 constant_dynamic-slice_fusion.3
  43.9 0.7 constant_dynamic-slice_fusion.3
  45.3 0.7 constant_dynamic-slice_fusion.3
  46.6 0.7 constant_dynamic-slice_fusion.3
  48.0 0.7 constant_dynamic-slice_fusion.3
  49.4 0.7 constant_dynamic-slice_fusion.3
  50.8 0.7 constant_dynamic-slice_fusion.3
  52.2 0.7 constant_dynamic-slice_fusion.3
  53.5 0.7 constant_dynamic-slice_fusion.3
  54.9 0.7 constant_dynamic-slice_fusion.3
  56.3 0.7 constant_dynamic-slice_fusion.3
  57.7 0.7 constant_dynamic-slice_fusion.3
  59.1 0.7 constant_dynamic-slice_fusion.3
  60.4 0.7 constant_dynamic-slice_fusion.3
  61.8 0.7 constant_dynamic-slice_fusion.3
  63.2 0.7 constant_dynamic-slice_fusion.3
  64.6 0.7 constant_dynamic-slice_fusion.3
  66.0 0.7 constant_dynamic-slice_fusion.3
  67.3 0.7 constant_dynamic-slice_fusion.3
  68.7 0.7 constant_dynamic-slice_fusion.3
  70.1 0.7 constant_dynamic-slice_fusion.3
  71.5 0.7 constant_dynamic-slice_fusion.3
  72.9 0.7 constant_dynamic-slice_fusion.3
  74.2 0.7 constant_dynamic-slice_fusion.3
  75.6 0.7 constant_dynamic-slice_fusion.3
  77.0 0.7 constant_dynamic-slice_fusion.3
  78.4 0.7 constant_dynamic-slice_fusion.3
  79.8 0.7 constant_dynamic-slice_fusion.3
  81.1 0.7 constant_dynamic-slice_fusion.3
  215.0 1.2 constant_dynamic-slice_fusion.1
  216.2 7.4 %collective-permute-start = (bf16[259,1024]{1,0:T(8,128)(2,1)S(1)}, bf16[259,1024]{1,0:T(8,128)(2,1)}, u32[]{:S(2)}, u32[]{:S(2)}) collective-permute-start(bf16[259,1024]{1,0:T(8,128)(2,1)S(1)} %constant_dynamic-slice_fusion.1), channel_id=1, source_target_pairs={{0,4},{4,8},{8,12},{12,16},{16,20},{20,24},{24,28},{28,32},{32,36}... | collective-permute-start | bytes 1591304 | tf_op jit(solution)/shard_map/ppermute | solution.py:10
  223.6 1.1 slice.41
  224.7 2.2 collective-permute-start.1
  227.0 8.2 %collective-permute-done.1 = bf16[256,1024]{1,0:T(8,128)(2,1)S(1)} collective-permute-done((bf16[256,1024]{1,0:T(8,128)(2,1)S(1)}, bf16[256,1024]{1,0:T(8,128)(2,1)S(1)}, u32[]{:S(2)}, u32[]{:S(2)}) %collective-permute-start.1) | collective-permute-done | bytes 524320 | tf_op jit(solution)/shard_map/ppermute | solution.py:10
  235.2 0.8 copy-done
  236.0 14.8 %concatenate.3 = bf16[1539,1024]{1,0:T(8,128)(2,1)S(1)} concatenate(bf16[259,1024]{1,0:T(8,128)(2,1)} %collective-permute-done, bf16[1024,1024]{1,0:T(8,128)(2,1)} %param.8, bf16[256,1024]{1,0:T(8,128)(2,1)} %copy-done), dimensions={0} | concatenate | bytes 6303744 | tf_op jit(solution)/shard_map/concatenate | solution.py:33
  250.8 3.4 gather_fusion
  254.1 2.4 broadcast_select_fusion
  256.6 0.7 all-gather.6.cloned.1.call-update
  258.2 52.7 %all-gather.4.cloned.1.call-done = bf16[515,4096]{1,0:T(8,128)(2,1)} async-done(((bf16[515,1024]{1,0:T(8,128)(2,1)}), bf16[515,4096]{1,0:T(8,128)(2,1)}) %all-gather.4.cloned.1.call-update) | async-done | bytes 4218896 | tf_op jit(solution)/shard_map/all_gather | solution.py:57
  310.8 154.9 %all-gather.6.cloned.1.call-done = bf16[4096,1280]{1,0:T(8,128)(2,1)} async-done(((bf16[32,1280]{1,0:T(8,128)(2,1)}), bf16[4096,1280]{1,0:T(8,128)(2,1)}) %all-gather.6.cloned.1.call-update) | async-done | bytes 10485776 | tf_op jit(solution)/shard_map/all_gather | solution.py:60
  465.8 10.9 %fusion = f32[515,1280]{1,0:T(8,128)S(1)} fusion(bf16[515,4096]{1,0:T(8,128)(2,1)} %all-gather.4.cloned.1.call-done, bf16[4096,1280]{1,0:T(8,128)(2,1)} %all-gather.6.cloned.1.call-done), kind=kOutput, calls=%fused_computation.3 | convolution fusion | flops 5401485312 | bytes 17341440 | tf_op jit(solution)/shard_map/dot_general | solution.py:58
  476.7 3.3 multiply_convert_fusion
  (121 shorter events, 65.4 us)
Async XLA Ops:
  6.5 304.3 %all-gather.4.cloned.1.call-start = ((), (), s32[]{:S(2)}) async-start(), calls=%async_computation | async-start | bytes 5324800 | tf_op jit(solution)/shard_map/all_gather | solution.py:57
  216.2 19.8 %collective-permute-start = (bf16[259,1024]{1,0:T(8,128)(2,1)S(1)}, bf16[259,1024]{1,0:T(8,128)(2,1)}, u32[]{:S(2)}, u32[]{:S(2)}) collective-permute-start(bf16[259,1024]{1,0:T(8,128)(2,1)S(1)} %constant_dynamic-slice_fusion.1), channel_id=1, source_target_pairs={{0,4},{4,8},{8,12},{12,16},{16,20},{20,24},{24,28},{28,32},{32,36}... | collective-permute-start | bytes 1591304 | tf_op jit(solution)/shard_map/ppermute | solution.py:10
  224.7 10.5 %collective-permute-start.1 = (bf16[256,1024]{1,0:T(8,128)(2,1)S(1)}, bf16[256,1024]{1,0:T(8,128)(2,1)S(1)}, u32[]{:S(2)}, u32[]{:S(2)}) collective-permute-start(bf16[256,1024]{1,0:T(8,128)(2,1)S(1)} %slice.41), channel_id=1, source_target_pairs={{4,0},{8,4},{12,8},{16,12},{20,16},{24,20},{28,24},{32,28},{36,32}... | collective-permute-start | bytes 1572872 | tf_op jit(solution)/shard_map/ppermute | solution.py:10
  235.2 0.8 copy-start
  254.1 3.2 copy-start.3
  254.1 3.9 copy-start.1
  256.6 209.2 %all-gather.6.cloned.1.call-start = ((), (), s32[]{:S(2)}) async-start(), calls=%async_computation.1 | async-start | bytes 10567680 | tf_op jit(solution)/shard_map/all_gather | solution.py:60
  258.2 218.6 %copy-start.2 = (f32[1280]{0:T(1024)S(1)}, f32[1280]{0:T(1024)}, u32[]{:S(2)}) copy-start(f32[1280]{0:T(1024)} %param.13) | copy-start | bytes 15364
Sparse Core Ops, SparseCore 0:
  256.7 54.0 all-gather.3
  313.9 151.7 all-gather.5
where the time goes:
time: 489 us; the launch traced here: 487 us
  waiting for transfers between devices  217 us (44%)
  local copies, waits for them, and re-layouts  108 us (22%)
  loops' own time  90.8 us (19%)
  blocking collectives  30.5 us (6%)
  between operations  14.2 us (3%)
  matrix products  10.9 us (2%)
  starting transfers between devices  9.63 us (2%)
  other arithmetic  6.33 us (1%)
    all_gather x1, waiting for transfers between devices, body(): lax.all_gather(in_weight, 'seq', axis=0, tiled=True)  155 us
    another operation x1, loops' own time, carried_in(): return lax.fori_loop(0, count - 1, turn, subtotal)  90.8 us
    dynamic_slice x127, local copies, waits for them, and re-layouts, turn(): longer = join(subtotal, pieces[position])  84.4 us
    all_gather x1, waiting for transfers between devices, body(): features = lax.all_gather(moved, 'ch', axis=1, tiled=True)  52.7 us
    unnamed x1, blocking collectives  30.5 us
    concatenate x1, local copies, waits for them, and re-layouts, move_rows(): buffer = jnp.concatenate([from_left, ingest, from_right], axis=0)  14.8 us
    dot_general x1, matrix products, body(): jnp.dot(features, lax.all_gather(in_weight, 'seq', axis=0, tiled=True), p...  10.9 us
  transfers between devices with their start and end apart: 4, of which 3 were waited for; matrix products, arithmetic and copies ran while one was open for 0% of the time, Pallas kernels for 0%

commit v1 on v0

v1 whole, which is shorter than its diff:
```python
import functools

import jax
import jax.numpy as jnp
from jax import lax
from jax.experimental import pallas as pl
from jax.experimental.pallas import tpu as pltpu
from jax.sharding import PartitionSpec as P

MESH = pl.DeviceIdType.MESH
F32 = jnp.float32
BF16 = jnp.bfloat16
NY, NX = 4, 4
PLANE = 2 * NY
LEAD = 16


def onehot(rows, columns, shift):
    q = lax.broadcasted_iota(jnp.int32, (rows, columns), 0)
    k = lax.broadcasted_iota(jnp.int32, (rows, columns), 1)
    return k - q == shift


def pick(mask):
    return jnp.where(mask, 1.0, 0.0).astype(BF16)


def dot(a, b):
    return jnp.dot(a, b, preferred_element_type=F32)


def names(nz):
    table, half = {}, nz // 2

    def add(*key):
        table[key] = len(table)

    for d in range(1, PLANE):
        add("c1", d)
    for d in range(1, nz):
        add("c2", d)
    add("pair")
    for h in range(2):
        add("tail", h)
        add("head", h)
        for r in range(4):
            add("xr", h, r)
            add("xl", h, r)
            add("xf", h, r)
    for d in range(1, NY):
        add("ya", d)
    for s in range(1, half + 1):
        for j in range(NY):
            add("ua", s, j)
            add("da", s, j)
        add("ub", s)
        add("db", s)
    for t in range(nz):
        add("yu", t)
        add("yd", t)
        add("yf", t)
        add("pass", t)
    return table


def kernel(nz, table, count_ref, lens_ref, taps_ref, bias_ref, ingest, weight, out,
           ing, tail_s, tail_r, head_r, wa, wb, feat, proj, keep, cnt1, cnt2,
           sel_t, sel_o, sel_b, sel_h, outv, lsem, ssem, rsem):
    half = nz // 2
    tokens = outv.shape[0]
    hrows = tokens // 2
    trows = hrows + LEAD
    unit = tokens // 4
    depth, ca = weight.shape[0], wa.shape[1]
    cb = wb.shape[1]
    hcols = feat.shape[2]
    pair_rows = 2 * depth
    plane_rows = PLANE * depth
    per_x = nz * plane_rows // NX

    s = lax.axis_index("seq")
    x = lax.axis_index("ch")
    core = lax.rem(s, 2)
    p = lax.rem(s, PLANE)
    y = p // 2
    z = s // PLANE
    count_devices = nz * PLANE

    def at(zz, yy, cc):
        return {"seq": (zz * NY + yy) * 2 + cc, "ch": x}

    def zof(d):
        return lax.rem(z + (d + 2 * nz), nz)

    def yof(d):
        return lax.rem(y + (d + 2 * NY), NY)

    def xof(d):
        return lax.rem(x + (d + 2 * NX), NX)

    right = {"seq": lax.rem(s + 1, count_devices), "ch": x}
    left = {"seq": lax.rem(s + count_devices - 1, count_devices), "ch": x}
    sibling = {"seq": s + 1 - 2 * core, "ch": x}
    far = {"seq": lax.rem(s + count_devices - 1 + 2 * core, count_devices), "ch": x}
    xright = {"seq": s, "ch": xof(1)}
    xleft = {"seq": s, "ch": xof(-1)}

    def blk(zz, yy):
        return pl.ds(pl.multiple_of((zz * NY + yy) * pair_rows, pair_rows), pair_rows)

    def plane(zz):
        return pl.ds(pl.multiple_of(zz * plane_rows, plane_rows), plane_rows)

    def rc(key, src, dst, device):
        i = table[key]
        return pltpu.make_async_remote_copy(
            src_ref=src, dst_ref=dst, send_sem=ssem.at[i], recv_sem=rsem.at[i],
            device_id=device, device_id_type=MESH)

    sent = {None: [], 0: [], 1: []}

    def send(who, make, *args):
        make(*args).start()
        sent[who].append((make, args))

    def c1(d):
        peer = lax.rem(p + d, PLANE)
        return rc(("c1", d), cnt1.at[0], cnt1.at[d], {"seq": z * PLANE + peer, "ch": x})

    def c2(d):
        return rc(("c2", d), cnt2.at[0], cnt2.at[d], {"seq": zof(d) * PLANE + p, "ch": x})

    mine = pl.ds(pl.multiple_of(s * depth, depth), depth)

    def pair_to0():
        return rc(("pair",), weight.at[:, 0:ca], wa.at[mine], sibling)

    def pair_to1():
        return rc(("pair",), weight.at[:, ca:], wb.at[mine], sibling)

    def tail(h):
        return rc(("tail", h), tail_s.at[h], tail_r.at[h], right)

    def head(h):
        return rc(("head", h), ingest.at[0:hrows, h * hcols:(h + 1) * hcols], head_r.at[h], left)

    def xrows(r):
        return pl.ds(0, LEAD + unit) if r == 0 else pl.ds(LEAD + r * unit, unit)

    def xcopy(kind, h, r, source, device):
        block = feat.at[source * 2 + h, xrows(r)]
        return rc((kind, h, r), block, block, device)

    def xr(h, r):
        return xcopy("xr", h, r, x, xright)

    def xl(h, r):
        return xcopy("xl", h, r, x, xleft)

    def xf(h, r):
        if r % 2 == 0:
            return xcopy("xf", h, r, xof(-1), xright)
        return xcopy("xf", h, r, xof(1), xleft)

    def ya(d):
        block = wa.at[blk(z, y)]
        return rc(("ya", d), block, block, at(z, yof(d), 0))

    def ua(st, j):
        block = wa.at[blk(zof(1 - st), yof(-j))]
        return rc(("ua", st, j), block, block, at(zof(1), y, 0))

    def da(st, j):
        block = wa.at[blk(zof(st - 1), yof(-j))]
        return rc(("da", st, j), block, block, at(zof(-1), y, 0))

    def part(zz, yy, piece):
        if piece is None:
            return blk(zz, yy)
        first = (zz * NY + yy) * pair_rows + piece * depth
        return pl.ds(pl.multiple_of(first, depth), depth)

    def ub(st):
        block = wb.at[part(zof(1 - st), y, 0 if st == half else None)]
        return rc(("ub", st), block, block, at(zof(1), y, 1))

    def db(st):
        block = wb.at[part(zof(st - 1), y, 1 if st == half else None)]
        return rc(("db", st), block, block, at(zof(-1), y, 1))

    def yu(t):
        block = wb.at[blk(zof(-t), y)]
        return rc(("yu", t), block, block, at(z, yof(1), 1))

    def yd(t):
        block = wb.at[blk(zof(-t), y)]
        return rc(("yd", t), block, block, at(z, yof(-1), 1))

    def yf(t):
        step = 1 if t % 2 == 0 else -1
        block = wb.at[blk(zof(-t), yof(-step))]
        return rc(("yf", t), block, block, at(z, yof(step), 1))

    def pass_a(t):
        block = wa.at[plane(zof(-t))]
        return rc(("pass", t), block, block, sibling)

    def pass_b(t):
        block = wb.at[plane(zof(-t))]
        return rc(("pass", t), block, block, sibling)

    def planes(st):
        return [st] if st in (0, half) else [st, nz - st]

    load = pltpu.make_async_copy(ingest, ing, lsem.at[0])
    load.start()

    def own_a():
        return pltpu.make_async_copy(weight.at[:, 0:ca], wa.at[mine], lsem.at[1])

    def own_b():
        return pltpu.make_async_copy(weight.at[:, ca:], wb.at[mine], lsem.at[1])

    @pl.when(core == 0)
    def _():
        own_a().start()

    @pl.when(core == 1)
    def _():
        own_b().start()

    barrier = pltpu.get_barrier_semaphore()
    friends = [{"seq": z * PLANE + lax.rem(p + d, PLANE), "ch": x} for d in range(1, PLANE)]
    friends += [{"seq": zof(d) * PLANE + p, "ch": x} for d in range(1, nz)]
    friends += [far, xright, xleft]
    for friend in friends:
        pl.semaphore_signal(barrier, inc=1, device_id=friend, device_id_type=MESH)

    count = count_ref[0]
    cnt1[0] = jnp.full(cnt1.shape[1:], count, jnp.int32)
    load.wait()
    tail_pick = pick(onehot(trows, ing.shape[0], count - trows))
    for h in range(2):
        tail_s[h] = dot(tail_pick, ing[:, h * hcols:(h + 1) * hcols]).astype(BF16)
    pl.semaphore_wait(barrier, len(friends))

    for d in range(1, PLANE):
        send(None, c1, d)

    @pl.when(core == 0)
    def _():
        send(0, pair_to1)

    @pl.when(core == 1)
    def _():
        send(1, pair_to0)

    send(None, tail, 0)
    send(None, head, 0)
    total = cnt1[0]
    inside = jnp.zeros_like(total)
    for d in range(1, PLANE):
        c1(d).wait_recv()
        total += cnt1[d]
        inside += jnp.where(lax.rem(p + PLANE - d, PLANE) < p, cnt1[d], 0)
    cnt2[0] = total
    for d in range(1, nz):
        send(None, c2, d)
    send(None, tail, 1)
    send(None, head, 1)

    @pl.when(core == 0)
    def _():
        own_a().wait()
        pair_to0().wait_recv()
        for d in range(1, NY):
            send(0, ya, d)
        send(0, ua, 1, 0)
        send(0, da, 1, 0)
        for j in range(1, NY):
            ya(j).wait_recv()
            if half > 1 or j < NY // 2:
                send(0, ua, 1, j)
            if half > 1 or j >= NY // 2:
                send(0, da, 1, j)
        send(0, pass_a, 0)

    @pl.when(core == 1)
    def _():
        own_b().wait()
        pair_to1().wait_recv()
        send(1, ub, 1)
        send(1, db, 1)
        send(1, yu, 0)
        send(1, yd, 0)

    for d in range(1, nz):
        c2(d).wait_recv()
        inside += jnp.where(lax.rem(z + nz - d, nz) < z, cnt2[d], 0)
    shift = s * tokens - inside[0:1, 0:1]
    top = pick(onehot(trows, trows + 2 * hrows, hrows + shift))
    sel_t[...] = top[:, :trows]
    sel_o[...] = top[:, trows:]
    slot = lax.broadcasted_iota(jnp.int32, (hrows, 3 * hrows), 1)
    sel_b[...] = pick(onehot(hrows, 3 * hrows, hrows + shift) & (slot < count))
    sel_h[...] = pick(onehot(hrows, hrows, hrows + shift - count))

    def assemble(h):
        tail(h).wait_recv()
        head(h).wait_recv()
        cols = slice(h * hcols, (h + 1) * hcols)
        spot = x * 2 + h
        feat[spot, 0:trows] = (
            dot(sel_t[...], tail_r[h]) + dot(sel_o[...], ing[0:2 * hrows, cols])).astype(BF16)
        feat[spot, trows:trows + hrows] = (
            dot(sel_b[...], ing[0:3 * hrows, cols]) + dot(sel_h[...], head_r[h])).astype(BF16)
        for r in range(4):
            send(None, xr, h, r)
            send(None, xl, h, r)

    def step_a(st):
        for j in range(NY):
            if st < half or j < NY // 2:
                ua(st, j).wait_recv()
            if st + 1 < half or (st + 1 == half and j < NY // 2):
                send(0, ua, st + 1, j)
            if st < half or j >= NY // 2:
                da(st, j).wait_recv()
            if st + 1 < half or (st + 1 == half and j >= NY // 2):
                send(0, da, st + 1, j)
        for t in planes(st):
            send(0, pass_a, t)

    def step_b(st):
        if st <= half:
            ub(st).wait_recv()
            if st < half:
                send(1, ub, st + 1)
            db(st).wait_recv()
            if st < half:
                send(1, db, st + 1)
            for t in planes(st):
                send(1, yu, t)
                send(1, yd, t)
        if 1 <= st <= half + 1:
            for t in planes(st - 1):
                yu(t).wait_recv()
                yd(t).wait_recv()
                send(1, yf, t)
        if 2 <= st <= half + 2:
            for t in planes(st - 2):
                yf(t).wait_recv()
                send(1, pass_b, t)

    units = [(h, r) for h in range(2) for r in range(4)]

    def xforward(h, r):
        xr(h, r).wait_recv()
        xl(h, r).wait_recv()
        send(None, xf, h, r)

    assemble(0)
    assemble(1)
    waiting = list(units)
    for st in range(1, half + 1):
        @pl.when(core == 0)
        def _():
            step_a(st)

        @pl.when(core == 1)
        def _():
            step_b(st)

        if st == 1:
            row = lax.broadcasted_iota(jnp.int32, (128, 128), 0)
            col = lax.broadcasted_iota(jnp.int32, (128, 128), 1)
            lens = lens_ref[...].astype(F32)
            lens_col = jnp.sum(jnp.where(row == col, lens, 0.0), axis=1, keepdims=True)
            starts = jnp.sum(jnp.where(row < col, lens_col, 0.0), axis=0, keepdims=True)
            places = (s * tokens + lax.broadcasted_iota(jnp.int32, (tokens, 128), 0)).astype(F32)
            since = places - starts
            age = jnp.min(jnp.where(since >= 0.0, since, 1e9), axis=1, keepdims=True)
            for lag in range(1, 4):
                keep[lag - 1] = jnp.broadcast_to(jnp.where(age >= lag, 1.0, 0.0), (tokens, 128))
        if st >= 2 and waiting:
            xforward(*waiting.pop(0))
    while waiting:
        xforward(*waiting.pop(0))

    @pl.when(core == 0)
    def _():
        for t in range(nz):
            pass_b(t).wait_recv()

    @pl.when(core == 1)
    def _():
        step_b(half + 1)
        step_b(half + 2)
        for t in range(nz):
            pass_a(t).wait_recv()

    def project(first, rows, rels, fresh, last):
        def columns(w, base, width, number):
            @pl.loop(0, number)
            def _(n):
                from_ = pl.ds(pl.multiple_of(n * width, width), width)
                to = pl.ds(pl.multiple_of(base + n * width, 128), width)
                value = None if fresh else proj[first:first + rows, to]
                for rel in rels:
                    source = xof(rel)
                    for h in range(2):
                        deep = pl.ds(pl.multiple_of(source * per_x + h * hcols, hcols), hcols)
                        term = dot(feat[source * 2 + h, first:first + rows], w[deep, from_])
                        value = term if value is None else value + term
                if last:
                    value = value.astype(BF16).astype(F32)
                proj[first:first + rows, to] = value

        width = min(256, ca)
        columns(wa, 0, width, ca // width)
        columns(wb, ca, width, cb // width)

    def activate(first, rows):
        block = min(64, rows)

        @pl.loop(0, rows // block)
        def _(n):
            base = pl.multiple_of(first + n * block, block)
            here = pl.ds(base, block)
            for c in range((ca + cb) // 128):
                cols = slice(c * 128, (c + 1) * 128)
                window = proj[pl.ds(pl.multiple_of(base + LEAD - 8, 8), block + 8), cols]
                value = bias_ref[:, cols] + taps_ref[0:1, cols] * window[8:]
                for lag in range(1, 4):
                    value += taps_ref[lag:lag + 1, cols] * window[8 - lag:8 - lag + block] * keep[lag - 1, here]
                outv[here, cols] = (value / (1.0 + jnp.exp(-value))).astype(BF16)

        rows_ = pl.ds(first, rows)
        copy = pltpu.make_async_copy(outv.at[rows_], out.at[rows_], lsem.at[2 + first // hrows])
        copy.start()
        return copy

    for h in range(2):
        for r in range(2):
            xf(h, r).wait_recv()
    project(0, trows, (0, -1, 1, 2), True, True)
    copy0 = activate(0, hrows)
    project(trows, hrows, (0, -1, 1), True, False)
    for h in range(2):
        for r in range(2, 4):
            xf(h, r).wait_recv()
    project(trows, hrows, (2,), False, True)
    copy1 = activate(hrows, hrows)

    for make, args in sent[None]:
        make(*args).wait_send()

    @pl.when(core == 0)
    def _():
        for make, args in sent[0]:
            make(*args).wait_send()

    @pl.when(core == 1)
    def _():
        for make, args in sent[1]:
            make(*args).wait_send()

    copy0.wait()
    copy1.wait()


def body(ingest, ingest_count, doc_lengths, in_weight, conv_weight, conv_bias, interpret=False):
    nz = lax.axis_size("seq") // PLANE
    table = names(nz)
    tokens = ingest.shape[0] // 2
    hrows, trows = tokens // 2, tokens // 2 + LEAD
    depth, channels = in_weight.shape
    features = ingest.shape[1]
    hcols = features // 2
    ca = channels * 2 // 5 // 128 * 128
    cb = channels - ca
    total_depth = nz * PLANE * depth
    vmem = pl.BlockSpec(memory_space=pltpu.VMEM)
    hbm = pl.BlockSpec(memory_space=pl.ANY)
    flops = 2 * tokens * total_depth * channels
    return pl.pallas_call(
        functools.partial(kernel, nz, table),
        out_shape=jax.ShapeDtypeStruct((tokens, channels), BF16),
        in_specs=[pl.BlockSpec(memory_space=pltpu.SMEM), vmem, vmem, vmem, hbm, hbm],
        out_specs=hbm,
        scratch_shapes=[
            pltpu.VMEM(ingest.shape, BF16),
            pltpu.VMEM((2, trows, hcols), BF16),
            pltpu.VMEM((2, trows, hcols), BF16),
            pltpu.VMEM((2, hrows, hcols), BF16),
            pltpu.VMEM((total_depth, ca), BF16),
            pltpu.VMEM((total_depth, cb), BF16),
            pltpu.VMEM((2 * NX, LEAD + tokens, hcols), BF16),
            pltpu.VMEM((LEAD + tokens, channels), F32),
            pltpu.VMEM((3, tokens, 128), F32),
            pltpu.VMEM((PLANE, 8, 128), jnp.int32),
            pltpu.VMEM((nz, 8, 128), jnp.int32),
            pltpu.VMEM((trows, trows), BF16),
            pltpu.VMEM((trows, 2 * hrows), BF16),
            pltpu.VMEM((hrows, 3 * hrows), BF16),
            pltpu.VMEM((hrows, hrows), BF16),
            pltpu.VMEM((tokens, channels), BF16),
            pltpu.SemaphoreType.DMA((4,)),
            pltpu.SemaphoreType.DMA((len(table),)),
            pltpu.SemaphoreType.DMA((len(table),)),
        ],
        compiler_params=pltpu.CompilerParams(
            collective_id=0, has_side_effects=True, vmem_limit_bytes=48 * 1024 * 1024),
        cost_estimate=pl.CostEstimate(flops=flops, bytes_accessed=20 << 20, transcendentals=tokens * channels),
    )(ingest_count, doc_lengths.reshape(1, -1), conv_weight, conv_bias.reshape(1, -1), ingest, in_weight)


def solution(mesh):
    placed = (P("seq", "ch"), P("seq"), P(), P("seq", "ch"), P(None, "ch"), P("ch"))
    return jax.shard_map(
        body, mesh=mesh, in_specs=placed, out_specs=P("seq", "ch"), check_vma=False
    )
```

time: 489 us -> 89.4 us (0.18)
  waiting for transfers between devices: 217 us -> 0 us
  local copies, waits for them, and re-layouts: 108 us -> 5.62 us
  loops' own time: 90.8 us -> 0 us
  Pallas kernels: 0 us -> 82.7 us
  blocking collectives: 30.5 us -> 0 us
  between operations: 14.2 us -> 0.67 us
  matrix products: 10.9 us -> 0 us
  starting transfers between devices: 9.63 us -> 0 us
  other arithmetic: 6.33 us -> 0 us
    all_gather x2 -> x0, waiting for transfers between devices: 208 us -> none  [the longest x1 155 us: body(): lax.all_gather(in_weight, 'seq', axis=0, tiled=True)]
    another operation x1 -> x0, loops' own time: 90.8 us -> none  [carried_in(): return lax.fori_loop(0, count - 1, turn, subtotal)]
    dynamic_slice x128 -> x0, local copies, waits for them, and re-layouts: 85.6 us -> none  [the longest x127 84.4 us: turn(): longer = join(subtotal, pieces[position])]
    pallas_call x0 -> x1, Pallas kernels: none -> 82.7 us  [body(): pl.pallas_call(functools.partial(kernel, nz, table), out_shape=jax.ShapeD...]
    unnamed x1 -> x0, blocking collectives: 30.5 us -> none
    concatenate x1 -> x0, local copies, waits for them, and re-layouts: 14.8 us -> none  [move_rows(): buffer = jnp.concatenate([from_left, ingest, from_right], axis=0)]
    dot_general x1 -> x0, matrix products: 10.9 us -> none  [body(): jnp.dot(features, lax.all_gather(in_weight, 'seq', axis=0, tiled=True), p...]
    ppermute x2 -> x0, starting transfers between devices: 9.59 us -> none  [shifted(): lax.ppermute(value, axis, [(source, source + steps) for source in range(i...]
  transfers between devices with their start and end apart: 4 -> 0, of which waited for: 3 -> 0; matrix products, arithmetic and copies ran while one was open for 0% -> 0% of each run, Pallas kernels for 0% -> 0%
where the time goes in v1:
time: 89.4 us; the launch traced here: 89 us
  Pallas kernels  82.7 us (93%)
  local copies, waits for them, and re-layouts  5.62 us (6%)
    pallas_call x1, Pallas kernels, body(): pl.pallas_call(functools.partial(kernel, nz, table), out_shape=jax.ShapeD...  82.7 us
    unnamed x9, local copies, waits for them, and re-layouts  4.92 us

profile of v1, /device:TPU:1, one launch (start us, length us, event | category | flops | bytes accessed | tf_op | source)
XLA Modules:
  0.0 89.0 jit_solution(3537143091345023130)
XLA Ops:
  0.7 0.7 reshape.7.bias_ref
  1.4 0.0 copy-start
  1.4 1.6 %copy-done = bf16[1024,1024]{1,0:T(8,128)(2,1)S(1)} copy-done((bf16[1024,1024]{1,0:T(8,128)(2,1)S(1)}, bf16[1024,1024]{1,0:T(8,128)(2,1)}, u32[]{:S(2)}) %copy-start) | copy-done | bytes 2097176
  2.9 0.0 copy-start.1
  2.9 0.9 copy-done.1
  3.8 0.0 copy-start.2
  3.8 0.7 copy-done.2
  4.6 0.0 copy-start.3
  4.6 0.7 copy-done.3
  5.2 82.7 %shard_map.64 = bf16[512,1280]{1,0:T(8,128)(2,1)S(1)} custom-call(s32[1]{0:T(128)S(6)} %copy.8.count_ref, s32[1,128]{1,0:T(1,128)S(1)} %bitcast.1, f32[4,1280]{1,0:T(4,128)S(1)} %copy-done.2, f32[1,1280]{1,0:T(1,128)S(1)} %reshape.7.bias_ref, bf16[1024,1024]{1,0:T(8,128)(2,1)S(1)} %copy-done, bf16[32,1280]{1,0:T(8,128)(2,1)S(1)} %copy-done.1), custom_call_target="tpu_custom_call" | custom-call | flops 5368709120 | bytes 20971520 | tf_op jit(solution)/shard_map/pallas_call | solution.py:486
  87.9 1.1 %copy.9 = bf16[512,1280]{1,0:T(8,128)(2,1)} copy(bf16[512,1280]{1,0:T(8,128)(2,1)S(1)} %shard_map.64) | data formatting | bytes 2621440
Async XLA Ops:
  1.4 1.6 %copy-start = (bf16[1024,1024]{1,0:T(8,128)(2,1)S(1)}, bf16[1024,1024]{1,0:T(8,128)(2,1)}, u32[]{:S(2)}) copy-start(bf16[1024,1024]{1,0:T(8,128)(2,1)} %ingest.1) | copy-start | bytes 6291460
  2.9 0.9 copy-start.1
  3.8 0.7 copy-start.2
  4.6 0.7 copy-start.3

commit v2 on v1

--- a/solution.py
+++ b/solution.py
@@ -37,7 +37,7 @@
 
     for d in range(1, PLANE):
         add("c1", d)
-    for d in range(1, nz):
+    for d in range(1, half):
         add("c2", d)
     add("pair")
     for h in range(2):
@@ -53,8 +53,9 @@
         for j in range(NY):
             add("ua", s, j)
             add("da", s, j)
-        add("ub", s)
-        add("db", s)
+        for piece in range(2):
+            add("ub", s, piece)
+            add("db", s, piece)
     for t in range(nz):
         add("yu", t)
         add("yd", t)
@@ -63,8 +64,8 @@
     return table
 
 
-def kernel(nz, table, count_ref, lens_ref, taps_ref, bias_ref, ingest, weight, out,
-           ing, tail_s, tail_r, head_r, wa, wb, feat, proj, keep, cnt1, cnt2,
+def kernel(nz, table, rows_total, count_hbm, lens_hbm, taps_hbm, bias_hbm, ingest, weight, out,
+           count_ref, lens_ref, taps_ref, bias_ref, ing, tail_s, tail_r, head_r, wa, wb, feat, proj, keep, cnt1, cnt2,
            sel_t, sel_o, sel_b, sel_h, outv, lsem, ssem, rsem):
     half = nz // 2
     tokens = outv.shape[0]
@@ -92,6 +93,11 @@
     def zof(d):
         return lax.rem(z + (d + 2 * nz), nz)
 
+    zlow = lax.rem(z, half)
+
+    def zpeer(d):
+        return z - zlow + lax.rem(zlow + d, half)
+
     def yof(d):
         return lax.rem(y + (d + 2 * NY), NY)
 
@@ -128,7 +134,7 @@
         return rc(("c1", d), cnt1.at[0], cnt1.at[d], {"seq": z * PLANE + peer, "ch": x})
 
     def c2(d):
-        return rc(("c2", d), cnt2.at[0], cnt2.at[d], {"seq": zof(d) * PLANE + p, "ch": x})
+        return rc(("c2", d), cnt2.at[0], cnt2.at[d], {"seq": zpeer(d) * PLANE + p, "ch": x})
 
     mine = pl.ds(pl.multiple_of(s * depth, depth), depth)
 
@@ -175,18 +181,19 @@
         return rc(("da", st, j), block, block, at(zof(-1), y, 0))
 
     def part(zz, yy, piece):
-        if piece is None:
-            return blk(zz, yy)
         first = (zz * NY + yy) * pair_rows + piece * depth
         return pl.ds(pl.multiple_of(first, depth), depth)
 
-    def ub(st):
-        block = wb.at[part(zof(1 - st), y, 0 if st == half else None)]
-        return rc(("ub", st), block, block, at(zof(1), y, 1))
-
-    def db(st):
-        block = wb.at[part(zof(st - 1), y, 1 if st == half else None)]
-        return rc(("db", st), block, block, at(zof(-1), y, 1))
+    def ub(st, piece):
+        block = wb.at[part(zof(1 - st), y, piece)]
+        return rc(("ub", st, piece), block, block, at(zof(1), y, 1))
+
+    def db(st, piece):
+        block = wb.at[part(zof(st - 1), y, piece)]
+        return rc(("db", st, piece), block, block, at(zof(-1), y, 1))
+
+    def goes(way, st, piece):
+        return st < half or (st == half and piece == way)
 
     def yu(t):
         block = wb.at[blk(zof(-t), y)]
@@ -213,6 +220,9 @@
         return [st] if st in (0, half) else [st, nz - st]
 
     load = pltpu.make_async_copy(ingest, ing, lsem.at[0])
+    small = [pltpu.make_async_copy(a, b, lsem.at[4 + i]) for i, (a, b) in enumerate(
+        ((count_hbm, count_ref), (lens_hbm, lens_ref), (taps_hbm, taps_ref), (bias_hbm, bias_ref)))]
+    small[0].start()
     load.start()
 
     def own_a():
@@ -230,33 +240,34 @@
         own_b().start()
 
     barrier = pltpu.get_barrier_semaphore()
-    friends = [{"seq": z * PLANE + lax.rem(p + d, PLANE), "ch": x} for d in range(1, PLANE)]
-    friends += [{"seq": zof(d) * PLANE + p, "ch": x} for d in range(1, nz)]
-    friends += [far, xright, xleft]
+    friends = [{"seq": zpeer(d) * PLANE + p, "ch": x} for d in range(1, half)]
+    friends += [at(zof(1), y, core), at(zof(-1), y, core), far, xright, xleft]
+    friends += [{"seq": z * PLANE + lax.rem(p + d, PLANE), "ch": x} for d in range(1, PLANE)]
     for friend in friends:
         pl.semaphore_signal(barrier, inc=1, device_id=friend, device_id_type=MESH)
-
+    for copy in small[1:]:
+        copy.start()
+    small[0].wait()
     count = count_ref[0]
     cnt1[0] = jnp.full(cnt1.shape[1:], count, jnp.int32)
+    pl.semaphore_wait(barrier, len(friends))
+
+    for d in range(1, PLANE):
+        send(None, c1, d)
+
+    @pl.when(core == 0)
+    def _():
+        send(0, pair_to1)
+
+    @pl.when(core == 1)
+    def _():
+        send(1, pair_to0)
+
+    send(None, head, 0)
     load.wait()
     tail_pick = pick(onehot(trows, ing.shape[0], count - trows))
-    for h in range(2):
-        tail_s[h] = dot(tail_pick, ing[:, h * hcols:(h + 1) * hcols]).astype(BF16)
-    pl.semaphore_wait(barrier, len(friends))
-
-    for d in range(1, PLANE):
-        send(None, c1, d)
-
-    @pl.when(core == 0)
-    def _():
-        send(0, pair_to1)
-
-    @pl.when(core == 1)
-    def _():
-        send(1, pair_to0)
-
+    tail_s[0] = dot(tail_pick, ing[:, 0:hcols]).astype(BF16)
     send(None, tail, 0)
-    send(None, head, 0)
     total = cnt1[0]
     inside = jnp.zeros_like(total)
     for d in range(1, PLANE):
@@ -264,39 +275,39 @@
         total += cnt1[d]
         inside += jnp.where(lax.rem(p + PLANE - d, PLANE) < p, cnt1[d], 0)
     cnt2[0] = total
-    for d in range(1, nz):
+    for d in range(1, half):
         send(None, c2, d)
-    send(None, tail, 1)
-    send(None, head, 1)
 
     @pl.when(core == 0)
     def _():
         own_a().wait()
         pair_to0().wait_recv()
+        send(0, ua, 1, 0)
+        send(0, da, 1, 0)
         for d in range(1, NY):
             send(0, ya, d)
-        send(0, ua, 1, 0)
-        send(0, da, 1, 0)
-        for j in range(1, NY):
-            ya(j).wait_recv()
-            if half > 1 or j < NY // 2:
-                send(0, ua, 1, j)
-            if half > 1 or j >= NY // 2:
-                send(0, da, 1, j)
-        send(0, pass_a, 0)
 
     @pl.when(core == 1)
     def _():
         own_b().wait()
         pair_to1().wait_recv()
-        send(1, ub, 1)
-        send(1, db, 1)
+        for piece in range(2):
+            for way, ring in enumerate((ub, db)):
+                if goes(way, 1, piece):
+                    send(1, ring, 1, piece)
         send(1, yu, 0)
         send(1, yd, 0)
 
-    for d in range(1, nz):
+    tail_s[1] = dot(tail_pick, ing[:, hcols:]).astype(BF16)
+    send(None, head, 1)
+    send(None, tail, 1)
+
+    group = cnt2[0]
+    for d in range(1, half):
         c2(d).wait_recv()
-        inside += jnp.where(lax.rem(z + nz - d, nz) < z, cnt2[d], 0)
+        group += cnt2[d]
+        inside += jnp.where(lax.rem(zlow + half - d, half) < zlow, cnt2[d], 0)
+    inside += jnp.where(z >= half, rows_total - group, 0)
     shift = s * tokens - inside[0:1, 0:1]
     top = pick(onehot(trows, trows + 2 * hrows, hrows + shift))
     sel_t[...] = top[:, :trows]
@@ -319,6 +330,15 @@
             send(None, xl, h, r)
 
     def step_a(st):
+        if st == 0:
+            for j in range(1, NY):
+                ya(j).wait_recv()
+                if half > 1 or j < NY // 2:
+                    send(0, ua, 1, j)
+                if half > 1 or j >= NY // 2:
+                    send(0, da, 1, j)
+            send(0, pass_a, 0)
+            return
         for j in range(NY):
             if st < half or j < NY // 2:
                 ua(st, j).wait_recv()
@@ -333,22 +353,22 @@
 
     def step_b(st):
         if st <= half:
-            ub(st).wait_recv()
-            if st < half:
-                send(1, ub, st + 1)
-            db(st).wait_recv()
-            if st < half:
-                send(1, db, st + 1)
+            for piece in range(2):
+                for way, ring in enumerate((ub, db)):
+                    if goes(way, st, piece):
+                        ring(st, piece).wait_recv()
+                    if goes(way, st + 1, piece):
+                        send(1, ring, st + 1, piece)
             for t in planes(st):
                 send(1, yu, t)
                 send(1, yd, t)
-        if 1 <= st <= half + 1:
-            for t in planes(st - 1):
+        if 2 <= st <= half + 2:
+            for t in planes(st - 2):
                 yu(t).wait_recv()
                 yd(t).wait_recv()
                 send(1, yf, t)
-        if 2 <= st <= half + 2:
-            for t in planes(st - 2):
+        if 3 <= st <= half + 3:
+            for t in planes(st - 3):
                 yf(t).wait_recv()
                 send(1, pass_b, t)
 
@@ -359,10 +379,16 @@
         xl(h, r).wait_recv()
         send(None, xf, h, r)
 
-    assemble(0)
-    assemble(1)
     waiting = list(units)
+
+    @pl.when(core == 0)
+    def _():
+        step_a(0)
+
     for st in range(1, half + 1):
+        if st <= 2:
+            assemble(st - 1)
+
         @pl.when(core == 0)
         def _():
             step_a(st)
@@ -371,7 +397,9 @@
         def _():
             step_b(st)
 
-        if st == 1:
+        if st == 3 or half < 3 and st == half:
+            for copy in small[1:]:
+                copy.wait()
             row = lax.broadcasted_iota(jnp.int32, (128, 128), 0)
             col = lax.broadcasted_iota(jnp.int32, (128, 128), 1)
             lens = lens_ref[...].astype(F32)
@@ -396,6 +424,7 @@
     def _():
         step_b(half + 1)
         step_b(half + 2)
+        step_b(half + 3)
         for t in range(nz):
             pass_a(t).wait_recv()
 
@@ -430,7 +459,7 @@
             for c in range((ca + cb) // 128):
                 cols = slice(c * 128, (c + 1) * 128)
                 window = proj[pl.ds(pl.multiple_of(base + LEAD - 8, 8), block + 8), cols]
-                value = bias_ref[:, cols] + taps_ref[0:1, cols] * window[8:]
+                value = bias_ref[cols].reshape(1, 128) + taps_ref[0:1, cols] * window[8:]
                 for lag in range(1, 4):
                     value += taps_ref[lag:lag + 1, cols] * window[8 - lag:8 - lag + block] * keep[lag - 1, here]
                 outv[here, cols] = (value / (1.0 + jnp.exp(-value))).astype(BF16)
@@ -469,7 +498,7 @@
     copy1.wait()
 
 
-def body(ingest, ingest_count, doc_lengths, in_weight, conv_weight, conv_bias, interpret=False):
+def body(ingest, ingest_count, doc_lengths, in_weight, conv_weight, conv_bias):
     nz = lax.axis_size("seq") // PLANE
     table = names(nz)
     tokens = ingest.shape[0] // 2
@@ -480,15 +509,18 @@
     ca = channels * 2 // 5 // 128 * 128
     cb = channels - ca
     total_depth = nz * PLANE * depth
-    vmem = pl.BlockSpec(memory_space=pltpu.VMEM)
-    hbm = pl.BlockSpec(memory_space=pl.ANY)
+    hbm = pl.BlockSpec(memory_space=pltpu.HBM)
     flops = 2 * tokens * total_depth * channels
     return pl.pallas_call(
-        functools.partial(kernel, nz, table),
+        functools.partial(kernel, nz, table, nz * PLANE * tokens),
         out_shape=jax.ShapeDtypeStruct((tokens, channels), BF16),
-        in_specs=[pl.BlockSpec(memory_space=pltpu.SMEM), vmem, vmem, vmem, hbm, hbm],
+        in_specs=[hbm] * 6,
         out_specs=hbm,
         scratch_shapes=[
+            pltpu.SMEM((1,), jnp.int32),
+            pltpu.VMEM((1, 128), jnp.int32),
+            pltpu.VMEM(conv_weight.shape, F32),
+            pltpu.VMEM(conv_bias.shape, F32),
             pltpu.VMEM(ingest.shape, BF16),
             pltpu.VMEM((2, trows, hcols), BF16),
             pltpu.VMEM((2, trows, hcols), BF16),
@@ -499,20 +531,20 @@
             pltpu.VMEM((LEAD + tokens, channels), F32),
             pltpu.VMEM((3, tokens, 128), F32),
             pltpu.VMEM((PLANE, 8, 128), jnp.int32),
-            pltpu.VMEM((nz, 8, 128), jnp.int32),
+            pltpu.VMEM((nz // 2, 8, 128), jnp.int32),
             pltpu.VMEM((trows, trows), BF16),
             pltpu.VMEM((trows, 2 * hrows), BF16),
             pltpu.VMEM((hrows, 3 * hrows), BF16),
             pltpu.VMEM((hrows, hrows), BF16),
             pltpu.VMEM((tokens, channels), BF16),
-            pltpu.SemaphoreType.DMA((4,)),
+            pltpu.SemaphoreType.DMA((8,)),
             pltpu.SemaphoreType.DMA((len(table),)),
             pltpu.SemaphoreType.DMA((len(table),)),
         ],
         compiler_params=pltpu.CompilerParams(
-            collective_id=0, has_side_effects=True, vmem_limit_bytes=48 * 1024 * 1024),
+            collective_id=0, has_side_effects=True, vmem_limit_bytes=60 * 1024 * 1024),
         cost_estimate=pl.CostEstimate(flops=flops, bytes_accessed=20 << 20, transcendentals=tokens * channels),
-    )(ingest_count, doc_lengths.reshape(1, -1), conv_weight, conv_bias.reshape(1, -1), ingest, in_weight)
+    )(ingest_count, doc_lengths.reshape(1, -1), conv_weight, conv_bias, ingest, in_weight)
 
 
 def solution(mesh):

time: 89.4 us -> 79.6 us (0.89)
  Pallas kernels: 82.7 us -> 76.3 us
  local copies, waits for them, and re-layouts: 5.62 us -> 2.46 us
    pallas_call x1, Pallas kernels: 82.7 us -> 76.3 us  [body(): pl.pallas_call(functools.partial(kernel, nz, table, nz * PLANE * tokens),...]
    unnamed x9 -> x1, local copies, waits for them, and re-layouts: 4.92 us -> 2.46 us
where the time goes in v2:
time: 79.6 us; the launch traced here: 79.4 us
  Pallas kernels  76.3 us (96%)
  local copies, waits for them, and re-layouts  2.46 us (3%)
    pallas_call x1, Pallas kernels, body(): pl.pallas_call(functools.partial(kernel, nz, table, nz * PLANE * tokens),...  76.3 us
    unnamed x1, local copies, waits for them, and re-layouts  2.46 us

profile of v2, /device:TPU:1, one launch (start us, length us, event | category | flops | bytes accessed | tf_op | source)
XLA Modules:
  0.0 79.4 jit_solution(9885814817879322669)
XLA Ops:
  0.7 76.3 %shard_map.64 = bf16[512,1280]{1,0:T(8,128)(2,1)} custom-call(s32[1]{0:T(128)S(6)} %copy.8.count_hbm, s32[1,128]{1,0:T(1,128)} %bitcast.1, f32[4,1280]{1,0:T(4,128)} %taps_hbm.1, f32[1280]{0:T(1024)} %bias_hbm.1, bf16[1024,1024]{1,0:T(8,128)(2,1)} %ingest.1, bf16[32,1280]{1,0:T(8,128)(2,1)} %weight.1), custom_call_target="tpu_custom_call" | custom-call | flops 5368709120 | bytes 20971520 | tf_op jit(solution)/shard_map/pallas_call | solution.py:514
  77.0 2.5 %copy.9 = bf16[512,1280]{1,0:T(8,128)(2,1)} copy(bf16[512,1280]{1,0:T(8,128)(2,1)} %shard_map.64) | data formatting | bytes 2621440

commit v3 on v2

--- a/solution.py
+++ b/solution.py
@@ -302,33 +302,6 @@
     send(None, head, 1)
     send(None, tail, 1)
 
-    group = cnt2[0]
-    for d in range(1, half):
-        c2(d).wait_recv()
-        group += cnt2[d]
-        inside += jnp.where(lax.rem(zlow + half - d, half) < zlow, cnt2[d], 0)
-    inside += jnp.where(z >= half, rows_total - group, 0)
-    shift = s * tokens - inside[0:1, 0:1]
-    top = pick(onehot(trows, trows + 2 * hrows, hrows + shift))
-    sel_t[...] = top[:, :trows]
-    sel_o[...] = top[:, trows:]
-    slot = lax.broadcasted_iota(jnp.int32, (hrows, 3 * hrows), 1)
-    sel_b[...] = pick(onehot(hrows, 3 * hrows, hrows + shift) & (slot < count))
-    sel_h[...] = pick(onehot(hrows, hrows, hrows + shift - count))
-
-    def assemble(h):
-        tail(h).wait_recv()
-        head(h).wait_recv()
-        cols = slice(h * hcols, (h + 1) * hcols)
-        spot = x * 2 + h
-        feat[spot, 0:trows] = (
-            dot(sel_t[...], tail_r[h]) + dot(sel_o[...], ing[0:2 * hrows, cols])).astype(BF16)
-        feat[spot, trows:trows + hrows] = (
-            dot(sel_b[...], ing[0:3 * hrows, cols]) + dot(sel_h[...], head_r[h])).astype(BF16)
-        for r in range(4):
-            send(None, xr, h, r)
-            send(None, xl, h, r)
-
     def step_a(st):
         if st == 0:
             for j in range(1, NY):
@@ -372,6 +345,37 @@
                 yf(t).wait_recv()
                 send(1, pass_b, t)
 
+    @pl.when(core == 1)
+    def _():
+        step_b(1)
+
+    group = cnt2[0]
+    for d in range(1, half):
+        c2(d).wait_recv()
+        group += cnt2[d]
+        inside += jnp.where(lax.rem(zlow + half - d, half) < zlow, cnt2[d], 0)
+    inside += jnp.where(z >= half, rows_total - group, 0)
+    shift = s * tokens - inside[0:1, 0:1]
+    top = pick(onehot(trows, trows + 2 * hrows, hrows + shift))
+    sel_t[...] = top[:, :trows]
+    sel_o[...] = top[:, trows:]
+    slot = lax.broadcasted_iota(jnp.int32, (hrows, 3 * hrows), 1)
+    sel_b[...] = pick(onehot(hrows, 3 * hrows, hrows + shift) & (slot < count))
+    sel_h[...] = pick(onehot(hrows, hrows, hrows + shift - count))
+
+    def assemble(h):
+        tail(h).wait_recv()
+        head(h).wait_recv()
+        cols = slice(h * hcols, (h + 1) * hcols)
+        spot = x * 2 + h
+        feat[spot, 0:trows] = (
+            dot(sel_t[...], tail_r[h]) + dot(sel_o[...], ing[0:2 * hrows, cols])).astype(BF16)
+        feat[spot, trows:trows + hrows] = (
+            dot(sel_b[...], ing[0:3 * hrows, cols]) + dot(sel_h[...], head_r[h])).astype(BF16)
+        for r in range(4):
+            send(None, xr, h, r)
+            send(None, xl, h, r)
+
     units = [(h, r) for h in range(2) for r in range(4)]
 
     def xforward(h, r):
@@ -395,7 +399,7 @@
 
         @pl.when(core == 1)
         def _():
-            step_b(st)
+            step_b(st + 1)
 
         if st == 3 or half < 3 and st == half:
             for copy in small[1:]:
@@ -422,7 +426,6 @@
 
     @pl.when(core == 1)
     def _():
-        step_b(half + 1)
         step_b(half + 2)
         step_b(half + 3)
         for t in range(nz):
@@ -445,9 +448,8 @@
                     value = value.astype(BF16).astype(F32)
                 proj[first:first + rows, to] = value
 
-        width = min(256, ca)
-        columns(wa, 0, width, ca // width)
-        columns(wb, ca, width, cb // width)
+        columns(wa, 0, ca, 1)
+        columns(wb, ca, cb, 1)
 
     def activate(first, rows):
         block = min(64, rows)
@@ -462,7 +464,8 @@
                 value = bias_ref[cols].reshape(1, 128) + taps_ref[0:1, cols] * window[8:]
                 for lag in range(1, 4):
                     value += taps_ref[lag:lag + 1, cols] * window[8 - lag:8 - lag + block] * keep[lag - 1, here]
-                outv[here, cols] = (value / (1.0 + jnp.exp(-value))).astype(BF16)
+                value = 0.5 * value
+                outv[here, cols] = (value + value * jnp.tanh(value)).astype(BF16)
 
         rows_ = pl.ds(first, rows)
         copy = pltpu.make_async_copy(outv.at[rows_], out.at[rows_], lsem.at[2 + first // hrows])

time: 79.6 us -> 78.1 us (0.981)
  Pallas kernels: 76.3 us -> 74.8 us
    pallas_call x1, Pallas kernels: 76.3 us -> 74.8 us  [body(): pl.pallas_call(functools.partial(kernel, nz, table, nz * PLANE * tokens),...]
where the time goes in v3:
time: 78.1 us; the launch traced here: 78 us
  Pallas kernels  74.8 us (96%)
  local copies, waits for them, and re-layouts  2.46 us (3%)
    pallas_call x1, Pallas kernels, body(): pl.pallas_call(functools.partial(kernel, nz, table, nz * PLANE * tokens),...  74.8 us
    unnamed x1, local copies, waits for them, and re-layouts  2.46 us

profile of v3, /device:TPU:1, one launch (start us, length us, event | category | flops | bytes accessed | tf_op | source)
XLA Modules:
  0.0 78.0 jit_solution(4913133625570497081)
XLA Ops:
  0.7 74.8 %shard_map.64 = bf16[512,1280]{1,0:T(8,128)(2,1)} custom-call(s32[1]{0:T(128)S(6)} %copy.8.count_hbm, s32[1,128]{1,0:T(1,128)} %bitcast.1, f32[4,1280]{1,0:T(4,128)} %taps_hbm.1, f32[1280]{0:T(1024)} %bias_hbm.1, bf16[1024,1024]{1,0:T(8,128)(2,1)} %ingest.1, bf16[32,1280]{1,0:T(8,128)(2,1)} %weight.1), custom_call_target="tpu_custom_call" | custom-call | flops 5368709120 | bytes 20971520 | tf_op jit(solution)/shard_map/pallas_call | solution.py:517
  75.5 2.5 %copy.9 = bf16[512,1280]{1,0:T(8,128)(2,1)} copy(bf16[512,1280]{1,0:T(8,128)(2,1)} %shard_map.64) | data formatting | bytes 2621440

commit v4 on v3

--- a/solution.py
+++ b/solution.py
@@ -419,10 +419,15 @@
     while waiting:
         xforward(*waiting.pop(0))
 
-    @pl.when(core == 0)
-    def _():
-        for t in range(nz):
-            pass_b(t).wait_recv()
+    def multiply(w, base):
+        value = None
+        for rel in (0, -1, 1):
+            source = xof(rel)
+            for h in range(2):
+                deep = pl.ds(pl.multiple_of(source * per_x + h * hcols, hcols), hcols)
+                term = dot(feat[source * 2 + h], w[deep])
+                value = term if value is None else value + term
+        proj[:, base:base + w.shape[1]] = value
 
     @pl.when(core == 1)
     def _():
@@ -431,25 +436,23 @@
         for t in range(nz):
             pass_a(t).wait_recv()
 
-    def project(first, rows, rels, fresh, last):
-        def columns(w, base, width, number):
-            @pl.loop(0, number)
-            def _(n):
-                from_ = pl.ds(pl.multiple_of(n * width, width), width)
-                to = pl.ds(pl.multiple_of(base + n * width, 128), width)
-                value = None if fresh else proj[first:first + rows, to]
-                for rel in rels:
-                    source = xof(rel)
-                    for h in range(2):
-                        deep = pl.ds(pl.multiple_of(source * per_x + h * hcols, hcols), hcols)
-                        term = dot(feat[source * 2 + h, first:first + rows], w[deep, from_])
-                        value = term if value is None else value + term
-                if last:
-                    value = value.astype(BF16).astype(F32)
-                proj[first:first + rows, to] = value
-
-        columns(wa, 0, ca, 1)
-        columns(wb, ca, cb, 1)
+    @pl.when(core == 0)
+    def _():
+        for t in range(nz):
+            pass_b(t).wait_recv()
+
+    multiply(wa, 0)
+    multiply(wb, ca)
+
+    def finish(first, rows):
+        source = xof(2)
+        for w, base in ((wa, 0), (wb, ca)):
+            to = slice(base, base + w.shape[1])
+            value = proj[first:first + rows, to]
+            for h in range(2):
+                deep = pl.ds(pl.multiple_of(source * per_x + h * hcols, hcols), hcols)
+                value += dot(feat[source * 2 + h, first:first + rows], w[deep])
+            proj[first:first + rows, to] = value.astype(BF16).astype(F32)
 
     def activate(first, rows):
         block = min(64, rows)
@@ -475,13 +478,12 @@
     for h in range(2):
         for r in range(2):
             xf(h, r).wait_recv()
-    project(0, trows, (0, -1, 1, 2), True, True)
+    finish(0, trows)
     copy0 = activate(0, hrows)
-    project(trows, hrows, (0, -1, 1), True, False)
     for h in range(2):
         for r in range(2, 4):
             xf(h, r).wait_recv()
-    project(trows, hrows, (2,), False, True)
+    finish(trows, hrows)
     copy1 = activate(hrows, hrows)
 
     for make, args in sent[None]:

time: 78.1 us -> 77.9 us (level)
  no operation moved by 1% of the time
where the time goes in v4:
time: 77.9 us; the launch traced here: 77.7 us
  Pallas kernels  74.6 us (96%)
  local copies, waits for them, and re-layouts  2.46 us (3%)
    pallas_call x1, Pallas kernels, body(): pl.pallas_call(functools.partial(kernel, nz, table, nz * PLANE * tokens),...  74.6 us
    unnamed x1, local copies, waits for them, and re-layouts  2.46 us

profile of v4, /device:TPU:1, one launch (start us, length us, event | category | flops | bytes accessed | tf_op | source)
XLA Modules:
  0.0 77.7 jit_solution(2805622687041898808)
XLA Ops:
  0.7 74.6 %shard_map.64 = bf16[512,1280]{1,0:T(8,128)(2,1)} custom-call(s32[1]{0:T(128)S(6)} %copy.8.count_hbm, s32[1,128]{1,0:T(1,128)} %bitcast.1, f32[4,1280]{1,0:T(4,128)} %taps_hbm.1, f32[1280]{0:T(1024)} %bias_hbm.1, bf16[1024,1024]{1,0:T(8,128)(2,1)} %ingest.1, bf16[32,1280]{1,0:T(8,128)(2,1)} %weight.1), custom_call_target="tpu_custom_call" | custom-call | flops 5368709120 | bytes 20971520 | tf_op jit(solution)/shard_map/pallas_call | solution.py:519
  75.3 2.5 %copy.9 = bf16[512,1280]{1,0:T(8,128)(2,1)} copy(bf16[512,1280]{1,0:T(8,128)(2,1)} %shard_map.64) | data formatting | bytes 2621440
